TPU v7x, 32 devices: a whole 2x2x4 slice. The times are simulated.
32 devices in a mesh: groups: 2 (over y), seq: 8 (over z, x), head: 2 (over core).
Axes of the slice: x: 2, y: 2, z: 4, core: 2. Of those that a mesh axis runs over, the one named last changes fastest.
Arguments:
- queries: bfloat16 [4096, 2048], P(('groups', 'seq'), 'head'), parts along dimension 0, may hold values from -24 to 24
- keys: bfloat16 [4096, 2048], P(('groups', 'seq'), 'head'), parts along dimension 0, may hold values from -24 to 24
- values: bfloat16 [4096, 2048], P(('groups', 'seq'), 'head'), parts along dimension 0, may hold values from -6 to 6
Outputs:
- attended: bfloat16 [4096, 2048], P(('groups', 'seq'), 'head'), parts along dimension 0
There are 2 independent parts, one for each index of `groups`. A program takes and returns all parts, laid end to end along the dimension named above; each array names one. Nothing has to cross between parts.
All inputs are finite; a program needn't handle non-finite values.
Results may differ from a plain program's by a relative error of at most 0.0057.
Values may be sent and summed in bfloat16 or wider, within the bound.
A program may use at most 64 MiB of HBM per device.

v0:
```python
import jax
import jax.numpy as jnp
from jax import lax
from jax.sharding import PartitionSpec as P

HEAD_DIM = 128
BLOCK = 128
MAX_LEVELS = 7


def extended(block, sides, width):
    for axis, dim in sides:
        count = lax.axis_size(axis)
        forward = [(i, i + 1) for i in range(count - 1)]
        backward = [(target, source) for source, target in forward]
        low = lax.ppermute(
            lax.slice_in_dim(block, block.shape[dim] - width, None, axis=dim), axis, forward
        )
        high = lax.ppermute(lax.slice_in_dim(block, 0, width, axis=dim), axis, backward)
        block = jnp.concatenate([low, block, high], axis=dim)
    return block


def swapped(x, axis, apart):
    return lax.ppermute(x, axis, [(i, i ^ 1 << apart) for i in range(lax.axis_size(axis))])


def pair_mean(x):
    shape = x.shape
    y = x.reshape(shape[:-3] + (shape[-3] // 2, 2) + shape[-2:]).astype(jnp.float32)
    return ((y[..., 0, :, :] + y[..., 1, :, :]) * 0.5).astype(jnp.bfloat16)


def attend(query_blk, key_blk, value_blk):
    scale = 1.0 / HEAD_DIM**0.5
    scores = (
        jnp.einsum("nqhe,nkhe->nqhk", query_blk, key_blk, preferred_element_type=jnp.float32)
        * scale
    )
    top = jnp.max(scores, axis=-1)
    probs = jnp.exp(scores - top[..., None])
    denom = jnp.sum(probs, axis=-1)
    numer = jnp.einsum(
        "nqhk,nkhe->nqhe", probs.astype(jnp.bfloat16), value_blk, preferred_element_type=jnp.float32
    )
    heads = query_blk.shape[2]
    return (top.reshape(-1, heads), denom.reshape(-1, heads), numer.reshape(-1, heads, HEAD_DIM))


def attend_near(query_blk, padded, keep):
    scale = 1.0 / HEAD_DIM**0.5
    parts = []
    for shift_blk in range(3):
        stop = padded.shape[1] - 2 + shift_blk
        parts.append(
            jnp.einsum(
                "nqhe,nkhe->nqhk",
                query_blk,
                padded[0, shift_blk:stop],
                preferred_element_type=jnp.float32,
            )
        )
    scores = jnp.concatenate(parts, axis=-1) * scale
    scores = jnp.where(keep[:, None, None, :], scores, -1e30)
    top = jnp.max(scores, axis=-1)
    probs = jnp.exp(scores - top[..., None])
    denom = jnp.sum(probs, axis=-1)
    probs_low = probs.astype(jnp.bfloat16)
    width_blk = query_blk.shape[1]
    numer = jnp.zeros(query_blk.shape, jnp.float32)
    for shift_blk in range(3):
        stop = padded.shape[1] - 2 + shift_blk
        numer = numer + jnp.einsum(
            "nqhk,nkhe->nqhe",
            probs_low[..., shift_blk * width_blk : (shift_blk + 1) * width_blk],
            padded[1, shift_blk:stop],
            preferred_element_type=jnp.float32,
        )
    heads = query_blk.shape[2]
    return (top.reshape(-1, heads), denom.reshape(-1, heads), numer.reshape(-1, heads, HEAD_DIM))


def on_device(queries, keys, values):
    rows, width = queries.shape
    heads = width // HEAD_DIM
    depth = (rows // BLOCK).bit_length() - 1
    nseq = lax.axis_size("seq")
    place = lax.axis_index("seq")
    levels = min(MAX_LEVELS, depth + nseq.bit_length() - 2)
    q_dev = queries.reshape(rows, heads, HEAD_DIM)
    kv_dev = jnp.stack([keys, values]).reshape(2, rows, heads, HEAD_DIM)
    count = rows // BLOCK
    padded = extended(kv_dev, (("seq", 1),), BLOCK)
    padded = padded.reshape(2, count + 2, BLOCK, heads, HEAD_DIM)
    blockid = jnp.arange(count)[:, None]
    column = jnp.arange(3 * BLOCK)[None, :]
    keep = jnp.logical_not(
        (place == 0) & (blockid == 0) & (column < BLOCK)
        | (place == nseq - 1) & (blockid == count - 1) & (column >= 2 * BLOCK)
    )
    results = [attend_near(q_dev.reshape(count, BLOCK, heads, HEAD_DIM), padded, keep)]
    chain_q = [q_dev]
    chain_kv = [kv_dev]
    for level in range(1, levels + 1):
        chain_q.append(pair_mean(chain_q[-1]))
        chain_kv.append(pair_mean(chain_kv[-1]))
    own = chain_kv[depth]
    for level in range(depth, levels + 1):
        bit = level - depth
        sibling = swapped(own, "seq", bit)
        qblk = chain_q[level].reshape(1, rows >> level, heads, HEAD_DIM)
        results.append(attend(qblk, sibling[0][None], sibling[1][None]))
        if level < levels:
            high = jnp.bitwise_and(jnp.right_shift(place, bit), 1) == 1
            lower = jnp.where(high, sibling, own)
            upper = jnp.where(high, own, sibling)
            own = pair_mean(jnp.concatenate([lower, upper], axis=1))
    state_top, state_den, state_num = results[-1]
    for level in range(len(results) - 2, -1, -1):
        top, denom, numer = results[level]
        coarse_top = jnp.repeat(state_top, 2, axis=0)
        coarse_den = jnp.repeat(state_den, 2, axis=0)
        coarse_num = jnp.repeat(state_num, 2, axis=0)
        highest = jnp.maximum(top, coarse_top)
        fine_weight = jnp.exp(top - highest)
        coarse_weight = 2.0 * jnp.exp(coarse_top - highest)
        state_top = highest
        state_den = fine_weight * denom + coarse_weight * coarse_den
        state_num = fine_weight[..., None] * numer + coarse_weight[..., None] * coarse_num
    return (state_num / state_den[..., None]).astype(jnp.bfloat16).reshape(rows, width)


def solution(mesh):
    in_specs = (
        P(("groups", "seq"), "head"),
        P(("groups", "seq"), "head"),
        P(("groups", "seq"), "head"),
    )
    out_specs = P(("groups", "seq"), "head")
    return jax.shard_map(
        on_device, mesh=mesh, in_specs=in_specs, out_specs=out_specs, check_vma=False
    )
```

profile of v0, /device:TPU:0, one launch (start us, length us, event | category | flops | bytes accessed | tf_op | source)
XLA Modules:
  0.0 102.6 jit_solution(11186642874756615979)
XLA Ops:
  0.0 1.2 %copy.165 = bf16[32,8,8,128]{3,2,1,0:T(8,128)(2,1)S(1)} copy(bf16[32,8,8,128]{3,1,2,0:T(8,128)(2,1)} %bitcast.214) | data formatting | bytes 1048576
  1.4 1.2 %fusion.65 = (bf16[2,128,8,128]{3,2,1,0:T(8,128)(2,1)}, bf16[2,128,8,128]{3,2,1,0:T(8,128)(2,1)}) fusion(bf16[2,256,8,128]{3,2,1,0:T(8,128)(2,1)S(1)} %bitcast_dynamic-update-slice_fusion), kind=kLoop, calls=%fused_computation.121 | loop fusion | bytes 2097152 | tf_op jit(solution)/shard_map/slice | solution.py:17
  2.7 5.6 %collective-permute-start = (bf16[2,128,8,128]{3,2,1,0:T(8,128)(2,1)}, bf16[2,128,8,128]{3,2,1,0:T(8,128)(2,1)}, u32[]{:S(2)}, u32[]{:S(2)}) collective-permute-start(bf16[2,128,8,128]{3,2,1,0:T(8,128)(2,1)} %get-tuple-element.32), channel_id=1, source_target_pairs={{0,2},{2,4},{4,6},{6,8},{8,10},{10,12},{12,14},{1,3},{3,5},{5,7},{... | collective-permute-start | bytes 1572872 | tf_op jit(solution)/shard_map/ppermute | solution.py:16
  8.3 1.3 %collective-permute-start.1 = (bf16[2,128,8,128]{3,2,1,0:T(8,128)(2,1)}, bf16[2,128,8,128]{3,2,1,0:T(8,128)(2,1)}, u32[]{:S(2)}, u32[]{:S(2)}) collective-permute-start(bf16[2,128,8,128]{3,2,1,0:T(8,128)(2,1)} %get-tuple-element.33), channel_id=1, source_target_pairs={{2,0},{4,2},{6,4},{8,6},{10,8},{12,10},{14,12},{3,1},{5,3},{7,5},{... | collective-permute-start | bytes 1572872 | tf_op jit(solution)/shard_map/ppermute | solution.py:19
  9.6 0.1 copy.110
  9.7 0.1 copy.111
  9.9 0.1 maximum_convert_fusion
  10.0 1.0 fusion.20
  11.0 2.6 %collective-permute-start.2 = (bf16[2,128,8,128]{3,1,2,0:T(8,128)(2,1)}, bf16[2,128,8,128]{3,1,2,0:T(8,128)(2,1)}, u32[]{:S(2)}, u32[]{:S(2)}) collective-permute-start(bf16[2,128,8,128]{3,1,2,0:T(8,128)(2,1)} %fusion.20), channel_id=1, source_target_pairs={{0,2},{2,0},{4,6},{6,4},{8,10},{10,8},{12,14},{14,12},{1,3},{3,1},... | collective-permute-start | bytes 1572872 | tf_op jit(solution)/shard_map/ppermute | solution.py:25
  13.6 0.1 convert_bitcast_fusion
  13.8 0.2 copy.170
  14.1 0.8 copy-done.5
  14.9 0.6 fusion.53
  15.7 1.9 %copy.167 = bf16[32,8,8,128]{3,2,1,0:T(8,128)(2,1)} copy(bf16[32,8,8,128]{3,1,2,0:T(8,128)(2,1)} %bitcast.209) | data formatting | bytes 1048576
  17.6 1.2 %fusion.70 = bf16[64,8,128]{2,1,0:T(8,128)(2,1)S(1)} fusion(f32[64,2,8,128]{3,2,1,0:T(8,128)} %copy-done.5), kind=kLoop, calls=%fused_computation.126 | loop fusion | flops 196608 | bytes 655360 | tf_op jit(solution)/shard_map/convert_element_type | solution.py:31
  18.8 12.5 %collective-permute-done = bf16[2,128,8,128]{3,2,1,0:T(8,128)(2,1)} collective-permute-done((bf16[2,128,8,128]{3,2,1,0:T(8,128)(2,1)}, bf16[2,128,8,128]{3,2,1,0:T(8,128)(2,1)}, u32[]{:S(2)}, u32[]{:S(2)}) %collective-permute-start) | collective-permute-done | bytes 524320 | tf_op jit(solution)/shard_map/ppermute | solution.py:16
  31.4 1.4 %pad_maximum_fusion = bf16[2,512,8,128]{3,2,1,0:T(8,128)(2,1)S(1)} fusion(bf16[2,128,8,128]{3,2,1,0:T(8,128)(2,1)} %collective-permute-done.1, bf16[2,256,8,128]{3,2,1,0:T(8,128)(2,1)S(1)} %copy-done.4, bf16[2,128,8,128]{3,2,1,0:T(8,128)(2,1)} %collective-permute-done), kind=kLoop, calls=%fused_computation.5 | loop fusion | flops 2097152 | bytes 4194304 | tf_op jit(solution)/shard_map/concatenate | solution.py:20
  32.8 1.3 %fusion.62 = (bf16[1,2,128,8,128]{4,3,2,1,0:T(8,128)(2,1)}, bf16[1,2,128,8,128]{4,3,2,1,0:T(8,128)(2,1)}, bf16[1,2,128,8,128]{4,3,2,1,0:T(8,128)(2,1)S(1)}, bf16...) fusion(bf16[2,4,128,8,128]{4,3,2,1,0:T(8,128)(2,1)S(1)} %bitcas, ...), kind=kLoop, calls=%fused_computation.118 | loop fusion | bytes 6291456 | tf_op jit(solution)/shard_map/slice | solution.py:76
  34.1 0.5 convolution_bitcast_fusion
  34.6 1.5 %convolution_bitcast_fusion.1 = f32[2,128,8,128]{1,3,2,0:T(8,128)} fusion(bf16[1,2,128,8,128]{4,3,2,1,0:T(8,128)(2,1)S(1)} %get-tuple-element.21, bf16[2,128,8,128]{3,2,1,0:T(8,128)(2,1)S(1)} %bitcast.196), kind=kOutput, calls=%fused_computation.10 | convolution fusion | flops 67108864 | bytes 2097152 | tf_op jit(solution)/shard_map/nqhe,nkhe->nqhk/dot_general | solution.py:56
  36.0 1.5 %convolution_bitcast_fusion.2 = f32[2,128,8,128]{1,3,2,0:T(8,128)} fusion(bf16[1,2,128,8,128]{4,3,2,1,0:T(8,128)(2,1)S(1)} %get-tuple-element.22, bf16[2,128,8,128]{3,2,1,0:T(8,128)(2,1)S(1)} %bitcast.197), kind=kOutput, calls=%fused_computation.11 | convolution fusion | flops 67108864 | bytes 2097152 | tf_op jit(solution)/shard_map/nqhe,nkhe->nqhk/dot_general | solution.py:56
  37.5 2.2 %copy.162 = bf16[1,2,128,8,128]{2,4,3,1,0:T(8,128)(2,1)} copy(bf16[1,2,128,8,128]{4,3,2,1,0:T(8,128)(2,1)} %get-tuple-element.19) | data formatting | bytes 1048576
  39.7 2.1 %copy.163 = bf16[1,2,128,8,128]{2,4,3,1,0:T(8,128)(2,1)} copy(bf16[1,2,128,8,128]{4,3,2,1,0:T(8,128)(2,1)} %get-tuple-element.23) | data formatting | bytes 1048576
  41.8 2.1 %copy.164 = bf16[1,2,128,8,128]{2,4,3,1,0:T(8,128)(2,1)} copy(bf16[1,2,128,8,128]{4,3,2,1,0:T(8,128)(2,1)} %get-tuple-element.18) | data formatting | bytes 1048576
  43.9 2.1 %fusion.17 = f32[2,128,8]{1,2,0:T(8,128)S(1)} fusion(f32[2,128,8,128]{1,3,2,0:T(8,128)S(1)} %convolution_bitcast_fusion, f32[2,128,8,128]{1,3,2,0:T(8,128)} %convolution_bitcast_fusion.1, f32[2,128,8,128]{1,3,2,0:T(8,128)} %convolution_bitcast_fusion.2, pred[2,384]{1,0:T(4,128)(4,1)S(1)} %or_not_fusion), kind=kLoop, calls=%fused_computation.41 | loop fusion | flops 3930112 | bytes 3154688 | tf_op jit(solution)/shard_map/reduce_max | solution.py:65
  46.1 1.7 %fusion.2 = (bf16[2,128,8,384]{1,3,2,0:T(8,128)(2,1)S(1)}, f32[2,128,8]{1,2,0:T(8,128)}) fusion(f32[2,128,8]{1,2,0:T(8,128)S(1)} %fusion.17, f32[2,128,8,128]{1,3,2,0:T(8,128)S(1)} %convolution_bitcast_fusion, f32[2,128,8,128]{1,3,2,0:T(8,128)S(1)} %copy-done, f32[2,128,8,128]{1,3,2,0:T(8,128)S(1)} %copy-done.1, pred[2,384]{1,0:T(4,128)(4,1)S(1)} %or_not_fusion), kind=kLoop, calls=%fused_computation.4 | loop fusion | flops 5502976 | bytes 4735744 | tf_op jit(solution)/shard_map/convert_element_type | solution.py:68
  47.8 1.4 %broadcast_select_fusion.3 = (bf16[2,128,8,128]{3,1,2,0:T(8,128)(2,1)S(1)}, bf16[2,128,8,128]{3,1,2,0:T(8,128)(2,1)S(1)}) fusion(bf16[2,128,8,128]{3,1,2,0:T(8,128)(2,1)} %collective-permute-done.2, pred[]{:T(512)S(6)} %eq.32, f32[2,128,2,8,128]{4,1,3,0,2:T(8,128)S(1)} %maximum_convert_fusion), kind=kLoop, calls=%fused_computation.64 | loop fusion | flops 1310720 | bytes 3670017 | tf_op jit(solution)/shard_map/jit(_where)/select_n | solution.py:115
  49.2 2.2 %fusion.64 = (f32[2,128,1,8,128]{4,2,1,3,0:T(1,128)S(1)}, f32[2,128,1,8,128]{4,2,1,3,0:T(1,128)S(1)}) fusion(bf16[2,128,2,8,128]{4,2,1,3,0:T(2,128)(2,1)S(1)} %bitcast.193), kind=kLoop, calls=%fused_computation.120 | loop fusion | bytes 4194304 | tf_op jit(solution)/shard_map/slice | solution.py:31
  51.5 0.1 fusion.18
  51.6 2.5 %collective-permute-start.3 = (bf16[2,128,8,128]{3,1,2,0:T(8,128)(2,1)S(1)}, bf16[2,128,8,128]{3,1,2,0:T(8,128)(2,1)S(1)}, u32[]{:S(2)}, u32[]{:S(2)}) collective-permute-start(bf16[2,128,8,128]{3,1,2,0:T(8,128)(2,1)S(1)} %fusion.18), channel_id=1, source_target_pairs={{0,4},{2,6},{4,0},{6,2},{8,12},{10,14},{12,8},{14,10},{1,5},{3,7},... | collective-permute-start | bytes 1572872 | tf_op jit(solution)/shard_map/ppermute | solution.py:25
  54.1 0.3 fusion.23
  54.4 0.3 convolution_add_fusion.1
  54.7 0.7 copy-done.9
  55.4 0.3 fusion.3
  55.7 0.4 copy.133
  56.1 10.0 %collective-permute-done.3 = bf16[2,128,8,128]{3,1,2,0:T(8,128)(2,1)S(1)} collective-permute-done((bf16[2,128,8,128]{3,1,2,0:T(8,128)(2,1)S(1)}, bf16[2,128,8,128]{3,1,2,0:T(8,128)(2,1)S(1)}, u32[]{:S(2)}, u32[]{:S(2)}) %collective-permute-start.3) | collective-permute-done | bytes 524320 | tf_op jit(solution)/shard_map/ppermute | solution.py:25
  66.2 0.2 maximum_convert_fusion.1
  66.4 1.2 %copy.116 = f32[2,256,8,128]{3,2,1,0:T(8,128)S(1)} copy(f32[2,256,8,128]{3,1,2,0:T(8,128)S(1)} %maximum_convert_fusion.1) | data formatting | bytes 4194304 | tf_op jit(solution)/shard_map/convert_element_type | solution.py:30
  67.6 0.1 fusion.63
  67.8 0.4 fusion.19
  68.2 2.8 %collective-permute-start.4 = (bf16[2,128,8,128]{3,1,2,0:T(8,128)(2,1)S(1)}, bf16[2,128,8,128]{3,1,2,0:T(8,128)(2,1)S(1)}, u32[]{:S(2)}, u32[]{:S(2)}) collective-permute-start(bf16[2,128,8,128]{3,1,2,0:T(8,128)(2,1)S(1)} %fusion.19), channel_id=1, source_target_pairs={{0,8},{2,10},{4,12},{6,14},{8,0},{10,2},{12,4},{14,6},{1,9},{3,11}... | collective-permute-start | bytes 1572872 | tf_op jit(solution)/shard_map/ppermute | solution.py:25
  71.0 1.3 %fusion.68 = (f32[128,8]{0,1:T(8,128)S(1)}, f32[1,128,8,128]{1,3,2,0:T(8,128)S(1)}) fusion(bf16[128,8,128]{2,1,0:T(8,128)(2,1)S(1)} %fusion.69, bf16[2,128,8,128]{3,1,2,0:T(8,128)(2,1)} %collective-permute-done.2), kind=kOutput, calls=%fused_computation.124 | convolution fusion | flops 33815552 | bytes 1052672 | tf_op jit(solution)/shard_map/nqhe,nkhe->nqhk/dot_general | solution.py:37
  72.3 0.4 fusion.67
  72.7 0.3 fusion.41
  73.0 20.6 %collective-permute-done.4 = bf16[2,128,8,128]{3,1,2,0:T(8,128)(2,1)S(1)} collective-permute-done((bf16[2,128,8,128]{3,1,2,0:T(8,128)(2,1)S(1)}, bf16[2,128,8,128]{3,1,2,0:T(8,128)(2,1)S(1)}, u32[]{:S(2)}, u32[]{:S(2)}) %collective-permute-start.4) | collective-permute-done | bytes 524320 | tf_op jit(solution)/shard_map/ppermute | solution.py:25
  93.6 0.8 copy-done.11
  94.4 0.3 fusion.66
  94.8 0.2 fusion.49
  95.2 1.2 %convolution_bitcast_fusion.5 = f32[32,8,128]{2,0,1:T(8,128)S(1)} fusion(bf16[2,128,8,128]{3,1,2,0:T(8,128)(2,1)} %copy-done.11, f32[1,32,8,128]{3,1,2,0:T(8,128)S(1)} %get-tuple-element.35, f32[32,8]{0,1:T(8,128)S(1)} %get-tuple-element.34), kind=kOutput, calls=%fused_computation.22 | convolution fusion | flops 8454144 | bytes 525312 | tf_op jit(solution)/shard_map/nqhk,nkhe->nqhe/dot_general | solution.py:43
  96.4 0.1 broadcast_in_dim.58
  96.5 0.3 fusion.8
  96.8 0.2 copy.140
  97.0 0.2 copy.141
  97.6 1.2 %fusion.5 = f32[128,8,128]{0,2,1:T(8,128)S(1)} fusion(f32[128,8,128]{0,2,1:T(8,128)S(1)} %copy.141, f32[1,128,8,128]{1,3,2,0:T(8,128)S(1)} %get-tuple-element.39, bf16[2,128,8,128]{3,1,2,0:T(8,128)(2,1)} %collective-permute-done.2, f32[128,8]{0,1:T(8,128)S(1)} %get-tuple-element.10, f32[128,8]{0,1:T(8,128)S(1)} %get-tuple-element.38, ...), kind=kOutput, calls=%fused_computation.14 | convolution fusion | flops 34209792 | bytes 1847296 | tf_op jit(solution)/shard_map/nqhk,nkhe->nqhe/dot_general | solution.py:43
  98.9 0.2 copy.142
  99.1 0.1 copy.124
  99.3 0.1 copy.147
  99.6 0.1 copy.126
  99.7 0.1 copy.135
  99.9 0.1 copy.149
  100.1 0.3 mul.221
  100.4 0.3 mul.226
  100.7 0.3 div.11
  101.1 1.5 %fusion.11 = bf16[256,1024]{1,0:T(8,128)(2,1)} fusion(f32[32,8,8,128]{3,2,1,0:T(8,128)S(1)} %bitcast.206, f32[32,8,8,128]{3,2,1,0:T(8,128)S(1)} %bitcast.203, f32[32,8,8,128]{3,2,1,0:T(8,128)S(1)} %bitcast.205, f32[32,8,8,128]{3,2,1,0:T(8,128)S(1)} %bitcast.202, f32[32,8,8,128]{3,2,1,0:T(8,128)S(1)} %bitcast.204), kind=kLoop, calls=%fused_computation.26 | loop fusion | flops 1310720 | bytes 5767168 | tf_op jit(solution)/shard_map/convert_element_type | solution.py:130
  (62 shorter events, 1.8 us)
Async XLA Ops:
  0.0 1.2 %copy-start.10 = (bf16[256,1024]{1,0:T(8,128)(2,1)S(1)}, bf16[256,1024]{1,0:T(8,128)(2,1)}, u32[]{:S(2)}) copy-start(bf16[256,1024]{1,0:T(8,128)(2,1)} %param.5) | copy-start | bytes 1572868
  1.4 8.4 %copy-start.3 = (bf16[2,256,8,128]{3,2,1,0:T(8,128)(2,1)}, bf16[2,256,8,128]{3,2,1,0:T(8,128)(2,1)S(1)}, u32[]{:S(2)}) copy-start(bf16[2,256,8,128]{3,2,1,0:T(8,128)(2,1)S(1)} %bitcast_dynamic-update-slice_fusion) | copy-start | bytes 3145732
  2.7 28.7 %collective-permute-start = (bf16[2,128,8,128]{3,2,1,0:T(8,128)(2,1)}, bf16[2,128,8,128]{3,2,1,0:T(8,128)(2,1)}, u32[]{:S(2)}, u32[]{:S(2)}) collective-permute-start(bf16[2,128,8,128]{3,2,1,0:T(8,128)(2,1)} %get-tuple-element.32), channel_id=1, source_target_pairs={{0,2},{2,4},{4,6},{6,8},{8,10},{10,12},{12,14},{1,3},{3,5},{5,7},{... | collective-permute-start | bytes 1572872 | tf_op jit(solution)/shard_map/ppermute | solution.py:16
  8.3 23.1 %collective-permute-start.1 = (bf16[2,128,8,128]{3,2,1,0:T(8,128)(2,1)}, bf16[2,128,8,128]{3,2,1,0:T(8,128)(2,1)}, u32[]{:S(2)}, u32[]{:S(2)}) collective-permute-start(bf16[2,128,8,128]{3,2,1,0:T(8,128)(2,1)} %get-tuple-element.33), channel_id=1, source_target_pairs={{2,0},{4,2},{6,4},{8,6},{10,8},{12,10},{14,12},{3,1},{5,3},{7,5},{... | collective-permute-start | bytes 1572872 | tf_op jit(solution)/shard_map/ppermute | solution.py:19
  10.0 3.6 %copy-start.6 = (bf16[256,1024]{1,0:T(8,128)(2,1)S(1)}, bf16[256,1024]{1,0:T(8,128)(2,1)}, u32[]{:S(2)}) copy-start(bf16[256,1024]{1,0:T(8,128)(2,1)} %param.3) | copy-start | bytes 1572868
  11.0 36.8 %collective-permute-start.2 = (bf16[2,128,8,128]{3,1,2,0:T(8,128)(2,1)}, bf16[2,128,8,128]{3,1,2,0:T(8,128)(2,1)}, u32[]{:S(2)}, u32[]{:S(2)}) collective-permute-start(bf16[2,128,8,128]{3,1,2,0:T(8,128)(2,1)} %fusion.20), channel_id=1, source_target_pairs={{0,2},{2,0},{4,6},{6,4},{8,10},{10,8},{12,14},{14,12},{1,3},{3,1},... | collective-permute-start | bytes 1572872 | tf_op jit(solution)/shard_map/ppermute | solution.py:25
  14.1 0.8 copy-start.5
  17.6 13.8 %copy-start.4 = (bf16[2,256,8,128]{3,2,1,0:T(8,128)(2,1)S(1)}, bf16[2,256,8,128]{3,2,1,0:T(8,128)(2,1)}, u32[]{:S(2)}) copy-start(bf16[2,256,8,128]{3,2,1,0:T(8,128)(2,1)} %copy-done.3) | copy-start | bytes 3145732
  32.8 1.3 %copy-start.2 = (bf16[32,8,8,128]{3,2,1,0:T(8,128)(2,1)S(1)}, bf16[32,8,8,128]{3,2,1,0:T(8,128)(2,1)}, u32[]{:S(2)}) copy-start(bf16[32,8,8,128]{3,2,1,0:T(8,128)(2,1)} %copy.167) | copy-start | bytes 1572868
  43.9 2.1 %copy-start = (f32[2,128,8,128]{1,3,2,0:T(8,128)S(1)}, f32[2,128,8,128]{1,3,2,0:T(8,128)}, u32[]{:S(2)}) copy-start(f32[2,128,8,128]{1,3,2,0:T(8,128)} %convolution_bitcast_fusion.1) | copy-start | bytes 3145732
  43.9 2.2 %copy-start.1 = (f32[2,128,8,128]{1,3,2,0:T(8,128)S(1)}, f32[2,128,8,128]{1,3,2,0:T(8,128)}, u32[]{:S(2)}) copy-start(f32[2,128,8,128]{1,3,2,0:T(8,128)} %convolution_bitcast_fusion.2) | copy-start | bytes 3145732
  51.4 2.6 %copy-start.7 = (bf16[1,2,128,8,128]{2,4,3,1,0:T(8,128)(2,1)S(1)}, bf16[1,2,128,8,128]{2,4,3,1,0:T(8,128)(2,1)}, u32[]{:S(2)}) copy-start(bf16[1,2,128,8,128]{2,4,3,1,0:T(8,128)(2,1)} %copy.162) | copy-start | bytes 1572868
  51.5 2.9 %copy-start.8 = (bf16[1,2,128,8,128]{2,4,3,1,0:T(8,128)(2,1)S(1)}, bf16[1,2,128,8,128]{2,4,3,1,0:T(8,128)(2,1)}, u32[]{:S(2)}) copy-start(bf16[1,2,128,8,128]{2,4,3,1,0:T(8,128)(2,1)} %copy.163) | copy-start | bytes 1572868
  51.6 14.5 %collective-permute-start.3 = (bf16[2,128,8,128]{3,1,2,0:T(8,128)(2,1)S(1)}, bf16[2,128,8,128]{3,1,2,0:T(8,128)(2,1)S(1)}, u32[]{:S(2)}, u32[]{:S(2)}) collective-permute-start(bf16[2,128,8,128]{3,1,2,0:T(8,128)(2,1)S(1)} %fusion.18), channel_id=1, source_target_pairs={{0,4},{2,6},{4,0},{6,2},{8,12},{10,14},{12,8},{14,10},{1,5},{3,7},... | collective-permute-start | bytes 1572872 | tf_op jit(solution)/shard_map/ppermute | solution.py:25
  54.4 1.0 %copy-start.9 = (bf16[1,2,128,8,128]{2,4,3,1,0:T(8,128)(2,1)S(1)}, bf16[1,2,128,8,128]{2,4,3,1,0:T(8,128)(2,1)}, u32[]{:S(2)}) copy-start(bf16[1,2,128,8,128]{2,4,3,1,0:T(8,128)(2,1)} %copy.164) | copy-start | bytes 1572868
  67.8 26.6 %copy-start.12 = (bf16[32,8,128]{2,1,0:T(8,128)(2,1)S(1)}, bf16[32,8,128]{2,1,0:T(8,128)(2,1)}, u32[]{:S(2)}) copy-start(bf16[32,8,128]{2,1,0:T(8,128)(2,1)} %fusion.53) | copy-start | bytes 196612
  68.2 25.4 %collective-permute-start.4 = (bf16[2,128,8,128]{3,1,2,0:T(8,128)(2,1)S(1)}, bf16[2,128,8,128]{3,1,2,0:T(8,128)(2,1)S(1)}, u32[]{:S(2)}, u32[]{:S(2)}) collective-permute-start(bf16[2,128,8,128]{3,1,2,0:T(8,128)(2,1)S(1)} %fusion.19), channel_id=1, source_target_pairs={{0,8},{2,10},{4,12},{6,14},{8,0},{10,2},{12,4},{14,6},{1,9},{3,11}... | collective-permute-start | bytes 1572872 | tf_op jit(solution)/shard_map/ppermute | solution.py:25
  93.6 0.8 copy-start.11
  97.3 2.3 %copy-start.13 = (f32[2,128,8]{1,2,0:T(8,128)S(1)}, f32[2,128,8]{1,2,0:T(8,128)}, u32[]{:S(2)}) copy-start(f32[2,128,8]{1,2,0:T(8,128)} %get-tuple-element.17) | copy-start | bytes 24580
where the time goes:
time: 103 us
  waiting for transfers between devices  43.1 us (42%)
  local copies, waits for them, and re-layouts  22.3 us (22%)
  starting transfers between devices  14.9 us (14%)
  other arithmetic  12.9 us (13%)
  matrix products  8.93 us (9%)
    ppermute x3, waiting for transfers between devices, swapped(): lax.ppermute(x, axis, [(i, i ^ 1 << apart) for i in range(lax.axis_size(a...  30.5 us
    ppermute x1, waiting for transfers between devices, extended(): lax.ppermute(lax.slice_in_dim(block, block.shape[dim] - width, None, axis...  12.5 us
    unnamed x36, local copies, waits for them, and re-layouts  12.2 us
    ppermute x3, starting transfers between devices, swapped(): lax.ppermute(x, axis, [(i, i ^ 1 << apart) for i in range(lax.axis_size(a...  7.94 us
    ppermute x1, starting transfers between devices, extended(): lax.ppermute(lax.slice_in_dim(block, block.shape[dim] - width, None, axis...  5.64 us
    convert_element_type x8, other arithmetic, pair_mean(): return ((y[..., 0, :, :] + y[..., 1, :, :]) * 0.5).astype(jnp.bfloat16)  3.42 us
    dot_general x3, matrix products, attend_near(): jnp.einsum('nqhe,nkhe->nqhk', query_blk, padded[0, shift_blk:stop], prefe...  3.4 us
    dot_general x3, matrix products, attend(): jnp.einsum('nqhk,nkhe->nqhe', probs.astype(jnp.bfloat16), value_blk, pref...  2.73 us
  transfers between devices with their start and end apart: 5, of which 3 were waited for; matrix products, arithmetic and copies ran while one was open for 25% of the time, Pallas kernels for 0%

commit v1 on v0

v1 whole, which is shorter than its diff:
```python
import functools
import math

import jax
import jax.numpy as jnp
from jax import lax
from jax.experimental import pallas as pl
from jax.experimental.pallas import tpu as pltpu
from jax.sharding import PartitionSpec as P

HEAD_DIM = 128
BLOCK = 128
MAX_LEVELS = 7
MESH = pl.DeviceIdType.MESH
RATE = math.log2(math.e) / math.sqrt(HEAD_DIM)


def softmax_part(scores, value):
    top = jnp.max(scores, axis=1, keepdims=True)
    probs = jnp.exp2((scores - top) * RATE).astype(jnp.bfloat16)
    wide = jnp.concatenate([value, jnp.ones_like(value)], axis=1)
    both = jnp.dot(probs, wide, preferred_element_type=jnp.float32)
    return top, both


def score(query, key):
    return lax.dot_general(
        query, key, (((1,), (1,)), ((), ())), preferred_element_type=jnp.float32
    )


def kernel(
    pairs, levels, local, q_in, k_in, v_in, out, kv, qbuf, obuf, kv1, own, sib,
    state, load_sem, kv_send, kv_recv, q_send, q_recv, halo_send, halo_recv,
    lev_send, lev_recv, out_local, out_send, out_recv,
):
    rows, width = q_in.shape
    half = width // 2
    heads = half // HEAD_DIM
    total = 2 * rows
    blocks = total // BLOCK
    place = lax.axis_index("seq")
    side = lax.rem(place, 2)
    other = 1 - side
    pair = place // 2
    partner = {"seq": pair * 2 + other}
    below = {"seq": lax.rem(pair + pairs - 1, pairs) * 2 + side}
    above = {"seq": lax.rem(pair + 1, pairs) * 2 + side}

    def mirror(level):
        apart = 1 << (level - local)
        bit = lax.rem(pair // apart, 2)
        return {"seq": (pair + apart - 2 * apart * bit) * 2 + side}

    barrier = pltpu.get_barrier_semaphore()
    peers = [partner, below, above] + [mirror(l) for l in range(local, levels + 1)]
    for peer in peers:
        pl.semaphore_signal(barrier, inc=1, device_id=peer, device_id_type=MESH)

    mine = pl.ds(pl.multiple_of(side * half, half), half)
    own_rows = pl.ds(pl.multiple_of(BLOCK + side * rows, BLOCK), rows)
    q_rows = pl.ds(pl.multiple_of(side * rows, BLOCK), rows)
    loads = [
        pltpu.make_async_copy(k_in.at[:, mine], kv.at[0, own_rows], load_sem.at[0]),
        pltpu.make_async_copy(v_in.at[:, mine], kv.at[1, own_rows], load_sem.at[1]),
        pltpu.make_async_copy(q_in.at[:, mine], qbuf.at[q_rows], load_sem.at[2]),
    ]
    for load in loads:
        load.start()
    pl.semaphore_wait(barrier, len(peers))

    def lanes(h):
        return pl.ds(pl.multiple_of(h * HEAD_DIM, HEAD_DIM), HEAD_DIM)

    def remote(src, dst, send, recv, device):
        return pltpu.make_async_remote_copy(
            src_ref=src, dst_ref=dst, send_sem=send, recv_sem=recv,
            device_id=device, device_id_type=MESH,
        )

    def theirs(h):
        return pl.ds(pl.multiple_of(other * half + h * HEAD_DIM, HEAD_DIM), HEAD_DIM)

    def send_k(h):
        return remote(k_in.at[:, theirs(h)], kv.at[0, own_rows, lanes(h)],
                      kv_send.at[0, h], kv_recv.at[0, h], partner)

    def send_v(h):
        return remote(v_in.at[:, theirs(h)], kv.at[1, own_rows, lanes(h)],
                      kv_send.at[1, h], kv_recv.at[1, h], partner)

    def send_q(h):
        return remote(q_in.at[:, theirs(h)], qbuf.at[q_rows, lanes(h)],
                      q_send.at[h], q_recv.at[h], partner)

    def send_down(h):
        return remote(kv.at[:, pl.ds(BLOCK, BLOCK), lanes(h)],
                      kv.at[:, pl.ds(BLOCK + total, BLOCK), lanes(h)],
                      halo_send.at[0, h], halo_recv.at[0, h], below)

    def send_up(h):
        return remote(kv.at[:, pl.ds(total, BLOCK), lanes(h)],
                      kv.at[:, pl.ds(0, BLOCK), lanes(h)],
                      halo_send.at[1, h], halo_recv.at[1, h], above)

    def send_level(level, h):
        at = level - local
        return remote(own.at[at, :, :, lanes(h)], sib.at[at, :, :, lanes(h)],
                      lev_send.at[at, h], lev_recv.at[at, h], mirror(level))

    def keep_out(h):
        cols = pl.ds(pl.multiple_of(side * half + h * HEAD_DIM, HEAD_DIM), HEAD_DIM)
        return pltpu.make_async_copy(
            obuf.at[q_rows, lanes(h)], out.at[:, cols], out_local.at[h])

    def send_out(h):
        cols = pl.ds(pl.multiple_of(side * half + h * HEAD_DIM, HEAD_DIM), HEAD_DIM)
        far = pl.ds(pl.multiple_of(other * rows, BLOCK), rows)
        return remote(obuf.at[far, lanes(h)], out.at[:, cols],
                      out_send.at[h], out_recv.at[h], partner)

    def each(body):
        @pl.loop(0, heads)
        def _(h):
            body(h)

    def start_kv(h):
        send_k(h).start()
        send_v(h).start()

    each(start_kv)
    each(lambda h: send_q(h).start())

    first, last = pair == 0, pair == pairs - 1

    @pl.when(first)
    def _():
        kv[:, pl.ds(0, BLOCK), :] = jnp.zeros((2, BLOCK, half), kv.dtype)

    @pl.when(last)
    def _():
        kv[:, pl.ds(BLOCK + total, BLOCK), :] = jnp.zeros((2, BLOCK, half), kv.dtype)

    loads[0].wait()
    loads[1].wait()

    def halo(h, here):
        @pl.when((side == here) & jnp.logical_not(first))
        def _():
            send_down(h).start()

        @pl.when((side == 1 - here) & jnp.logical_not(last))
        def _():
            send_up(h).start()

    each(lambda h: halo(h, 0))

    rowid = lax.broadcasted_iota(jnp.int32, (BLOCK, 2 * BLOCK), 0)
    colid = lax.broadcasted_iota(jnp.int32, (BLOCK, 2 * BLOCK), 1)
    averaging = jnp.where((colid >> 1) == rowid, 0.5, 0.0).astype(jnp.bfloat16)

    def mean(x):
        count = x.shape[0]
        parts = []
        for at in range(0, count, 2 * BLOCK):
            size = min(2 * BLOCK, count - at)
            parts.append(
                jnp.dot(averaging[: size // 2, :size], x[at : at + size],
                        preferred_element_type=jnp.float32).astype(jnp.bfloat16)
            )
        return parts[0] if len(parts) == 1 else jnp.concatenate(parts, axis=0)

    def coarsen(h):
        send_k(h).wait_recv()
        send_v(h).wait_recv()
        halo(h, 1)
        both = jnp.concatenate(
            [kv[0, pl.ds(BLOCK, total), lanes(h)], kv[1, pl.ds(BLOCK, total), lanes(h)]],
            axis=1)
        offset = 0
        for level in range(1, local):
            both = mean(both)
            count = total >> level
            for t in range(2):
                kv1[t, pl.ds(offset, count), lanes(h)] = both[:, t * HEAD_DIM : (t + 1) * HEAD_DIM]
            offset += count
        both = mean(both)
        for t in range(2):
            own[0, t, :, lanes(h)] = both[:, t * HEAD_DIM : (t + 1) * HEAD_DIM]
        send_level(local, h).start()

    each(coarsen)

    for level in range(local, levels):
        at = level - local

        def climb(h, level=level, at=at):
            send_level(level, h).wait_recv()
            for t in range(2):
                joined = jnp.concatenate([own[at, t, :, lanes(h)], sib[at, t, :, lanes(h)]], axis=0)
                own[at + 1, t, :, lanes(h)] = mean(joined)
            send_level(level + 1, h).start()

        each(climb)

    loads[2].wait()

    def attend(h):
        send_q(h).wait_recv()
        send_level(levels, h).wait_recv()

        @pl.when(jnp.logical_not(last))
        def _():
            send_down(h).wait_recv()

        @pl.when(jnp.logical_not(first))
        def _():
            send_up(h).wait_recv()

        queries = [qbuf[:, lanes(h)]]
        for level in range(1, levels + 1):
            queries.append(mean(queries[-1]))

        found = None
        for level in range(levels, -1, -1):
            count = total >> level
            if level >= local:
                at = level - local
                tops, both = softmax_part(
                    score(queries[level], sib[at, 0, :, lanes(h)]), sib[at, 1, :, lanes(h)])
                pieces = [(0, count, tops, both)]
            elif level >= 1:
                offset = sum(total >> l for l in range(1, level))
                pieces = []
                for b in range(count // BLOCK):
                    near = pl.ds(offset + (b ^ 1) * BLOCK, BLOCK)
                    tops, both = softmax_part(
                        score(queries[level][b * BLOCK : (b + 1) * BLOCK], kv1[0, near, lanes(h)]),
                        kv1[1, near, lanes(h)])
                    pieces.append((b * BLOCK, BLOCK, tops, both))
            else:
                pieces = []
                for b in range(blocks):
                    window = pl.ds(b * BLOCK, 3 * BLOCK)
                    s = score(queries[0][b * BLOCK : (b + 1) * BLOCK], kv[0, window, lanes(h)])
                    if b == 0:
                        s = jnp.concatenate(
                            [jnp.where(first, -1e30, s[:, :BLOCK]), s[:, BLOCK:]], axis=1)
                    if b == blocks - 1:
                        s = jnp.concatenate(
                            [s[:, : 2 * BLOCK], jnp.where(last, -1e30, s[:, 2 * BLOCK :])], axis=1)
                    tops, both = softmax_part(s, kv[1, window, lanes(h)])
                    pieces.append((b * BLOCK, BLOCK, tops, both))
            for start, size, tops, both in pieces:
                num, den = both[:, :HEAD_DIM], both[:, HEAD_DIM:]
                top = jnp.broadcast_to(tops, (size, HEAD_DIM))
                if level < levels:
                    span = pl.ds(start, size)
                    coarse_top = state[level, 0, span, :]
                    highest = jnp.maximum(top, coarse_top)
                    fine_weight = jnp.exp2((top - highest) * RATE)
                    coarse_weight = 2.0 * jnp.exp2((coarse_top - highest) * RATE)
                    top = highest
                    den = fine_weight * den + coarse_weight * state[level, 1, span, :]
                    num = fine_weight * num + coarse_weight * state[level, 2, span, :]
                if level == 0:
                    obuf[pl.ds(start, size), lanes(h)] = (num / den).astype(obuf.dtype)
                else:
                    for at, x in enumerate((top, den, num)):
                        for odd in range(2):
                            state[level - 1, at, pl.ds(2 * start + odd, size, stride=2), :] = x
        keep_out(h).start()
        send_out(h).start()

    each(attend)

    def finish(h):
        send_k(h).wait_send()
        send_v(h).wait_send()
        send_q(h).wait_send()
        for level in range(local, levels + 1):
            send_level(level, h).wait_send()

        @pl.when(jnp.logical_not(first))
        def _():
            send_down(h).wait_send()

        @pl.when(jnp.logical_not(last))
        def _():
            send_up(h).wait_send()

        keep_out(h).wait()
        send_out(h).wait()

    each(finish)


def on_device(queries, keys, values):
    rows, width = queries.shape
    half = width // 2
    heads = half // HEAD_DIM
    total = 2 * rows
    nseq = lax.axis_size("seq")
    pairs = nseq // 2
    depth = (rows // BLOCK).bit_length() - 1
    levels = min(MAX_LEVELS, depth + nseq.bit_length() - 2)
    local = depth + 1
    far = levels - local + 1
    coarse = sum(total >> l for l in range(1, local))
    bf16 = jnp.bfloat16
    dma = pltpu.SemaphoreType.DMA
    return pl.pallas_call(
        functools.partial(kernel, pairs, levels, local),
        out_shape=jax.ShapeDtypeStruct((rows, width), bf16),
        in_specs=[pl.BlockSpec(memory_space=pl.ANY)] * 3,
        out_specs=pl.BlockSpec(memory_space=pl.ANY),
        scratch_shapes=[
            pltpu.VMEM((2, total + 2 * BLOCK, half), bf16),
            pltpu.VMEM((total, half), bf16),
            pltpu.VMEM((total, half), bf16),
            pltpu.VMEM((2, coarse, half), bf16),
            pltpu.VMEM((far, 2, BLOCK, half), bf16),
            pltpu.VMEM((far, 2, BLOCK, half), bf16),
            pltpu.VMEM((levels, 3, total, HEAD_DIM), jnp.float32),
            dma((3,)),
            dma((2, heads)),
            dma((2, heads)),
            dma((heads,)),
            dma((heads,)),
            dma((2, heads)),
            dma((2, heads)),
            dma((far, heads)),
            dma((far, heads)),
            dma((heads,)),
            dma((heads,)),
            dma((heads,)),
        ],
        compiler_params=pltpu.CompilerParams(
            collective_id=0, has_side_effects=True, vmem_limit_bytes=40 * 2**20
        ),
    )(queries, keys, values)


def solution(mesh):
    spec = P(("groups", "seq"), "head")
    return jax.shard_map(
        on_device, mesh=mesh, in_specs=(spec, spec, spec), out_specs=spec, check_vma=False
    )
```

time: 103 us -> 45.5 us (0.44)
  waiting for transfers between devices: 43.1 us -> 0 us
  Pallas kernels: 0 us -> 41.3 us
  local copies, waits for them, and re-layouts: 22.3 us -> 3.92 us
  starting transfers between devices: 14.9 us -> 0 us
  other arithmetic: 12.9 us -> 0 us
  matrix products: 8.93 us -> 0 us
    ppermute x5 -> x0, waiting for transfers between devices: 43.1 us -> none  [the longest x3 30.5 us: swapped(): lax.ppermute(x, axis, [(i, i ^ 1 << apart) for i in range(lax.axis_size(a...]
    pallas_call x0 -> x1, Pallas kernels: none -> 41.3 us  [on_device(): pl.pallas_call(functools.partial(kernel, pairs, levels, local), out_shape...]
    ppermute x5 -> x0, starting transfers between devices: 14.9 us -> none  [the longest x3 7.94 us: swapped(): lax.ppermute(x, axis, [(i, i ^ 1 << apart) for i in range(lax.axis_size(a...]
    dot_general x12 -> x0, matrix products: 8.93 us -> none  [the longest x3 3.4 us: attend_near(): jnp.einsum('nqhe,nkhe->nqhk', query_blk, padded[0, shift_blk:stop], prefe...]
    unnamed x36 -> x7, local copies, waits for them, and re-layouts: 12.2 us -> 3.92 us
    convert_element_type x14 -> x0, other arithmetic: 7.06 us -> none  [the longest x8 3.42 us: pair_mean(): return ((y[..., 0, :, :] + y[..., 1, :, :]) * 0.5).astype(jnp.bfloat16)]
    slice x4 -> x0, local copies, waits for them, and re-layouts: 4.82 us -> none  [the longest x2 2.33 us: pair_mean(): return ((y[..., 0, :, :] + y[..., 1, :, :]) * 0.5).astype(jnp.bfloat16)]
    reduce_max x1 -> x0, other arithmetic: 2.12 us -> none  [attend_near(): top = jnp.max(scores, axis=-1)]
  transfers between devices with their start and end apart: 5 -> 0, of which waited for: 3 -> 0; matrix products, arithmetic and copies ran while one was open for 25% -> 0% of each run, Pallas kernels for 0% -> 0%
where the time goes in v1:
time: 45.5 us; the launch traced here: 45.3 us
  Pallas kernels  41.3 us (91%)
  local copies, waits for them, and re-layouts  3.92 us (9%)
    pallas_call x1, Pallas kernels, on_device(): pl.pallas_call(functools.partial(kernel, pairs, levels, local), out_shape...  41.3 us
    unnamed x7, local copies, waits for them, and re-layouts  3.92 us

profile of v1, /device:TPU:0, one launch (start us, length us, event | category | flops | bytes accessed | tf_op | source)
XLA Modules:
  0.0 45.3 jit_solution(11181281510300148114)
XLA Ops:
  0.0 0.0 copy-start
  0.0 1.0 %copy-done = bf16[256,1024]{1,0:T(8,128)(2,1)S(1)} copy-done((bf16[256,1024]{1,0:T(8,128)(2,1)S(1)}, bf16[256,1024]{1,0:T(8,128)(2,1)}, u32[]{:S(2)}) %copy-start) | copy-done | bytes 524312
  1.0 0.0 copy-start.1
  1.0 1.0 %copy-done.1 = bf16[256,1024]{1,0:T(8,128)(2,1)S(1)} copy-done((bf16[256,1024]{1,0:T(8,128)(2,1)S(1)}, bf16[256,1024]{1,0:T(8,128)(2,1)}, u32[]{:S(2)}) %copy-start.1) | copy-done | bytes 524312
  2.1 0.0 copy-start.2
  2.1 1.0 %copy-done.2 = bf16[256,1024]{1,0:T(8,128)(2,1)S(1)} copy-done((bf16[256,1024]{1,0:T(8,128)(2,1)S(1)}, bf16[256,1024]{1,0:T(8,128)(2,1)}, u32[]{:S(2)}) %copy-start.2) | copy-done | bytes 524312
  3.1 41.3 %shard_map.37 = bf16[256,1024]{1,0:T(8,128)(2,1)S(1)} custom-call(bf16[256,1024]{1,0:T(8,128)(2,1)S(1)} %copy-done, bf16[256,1024]{1,0:T(8,128)(2,1)S(1)} %copy-done.1, bf16[256,1024]{1,0:T(8,128)(2,1)S(1)} %copy-done.2), custom_call_target="tpu_custom_call" | custom-call | tf_op jit(solution)/shard_map/pallas_call | solution.py:312
  44.5 0.8 %copy.5 = bf16[256,1024]{1,0:T(8,128)(2,1)} copy(bf16[256,1024]{1,0:T(8,128)(2,1)S(1)} %shard_map.37) | data formatting | bytes 1048576
Async XLA Ops:
  0.0 1.0 %copy-start = (bf16[256,1024]{1,0:T(8,128)(2,1)S(1)}, bf16[256,1024]{1,0:T(8,128)(2,1)}, u32[]{:S(2)}) copy-start(bf16[256,1024]{1,0:T(8,128)(2,1)} %q_in.1) | copy-start | bytes 1572868
  1.0 1.0 %copy-start.1 = (bf16[256,1024]{1,0:T(8,128)(2,1)S(1)}, bf16[256,1024]{1,0:T(8,128)(2,1)}, u32[]{:S(2)}) copy-start(bf16[256,1024]{1,0:T(8,128)(2,1)} %k_in.1) | copy-start | bytes 1572868
  2.1 1.0 %copy-start.2 = (bf16[256,1024]{1,0:T(8,128)(2,1)S(1)}, bf16[256,1024]{1,0:T(8,128)(2,1)}, u32[]{:S(2)}) copy-start(bf16[256,1024]{1,0:T(8,128)(2,1)} %v_in.1) | copy-start | bytes 1572868

commit v2 on v1

--- a/solution.py
+++ b/solution.py
@@ -13,14 +13,6 @@
 MAX_LEVELS = 7
 MESH = pl.DeviceIdType.MESH
 RATE = math.log2(math.e) / math.sqrt(HEAD_DIM)
-
-
-def softmax_part(scores, value):
-    top = jnp.max(scores, axis=1, keepdims=True)
-    probs = jnp.exp2((scores - top) * RATE).astype(jnp.bfloat16)
-    wide = jnp.concatenate([value, jnp.ones_like(value)], axis=1)
-    both = jnp.dot(probs, wide, preferred_element_type=jnp.float32)
-    return top, both
 
 
 def score(query, key):
@@ -44,8 +36,9 @@
     other = 1 - side
     pair = place // 2
     partner = {"seq": pair * 2 + other}
-    below = {"seq": lax.rem(pair + pairs - 1, pairs) * 2 + side}
-    above = {"seq": lax.rem(pair + 1, pairs) * 2 + side}
+    first, last = pair == 0, pair == pairs - 1
+    below = {"seq": jnp.maximum(pair - 1, 0) * 2 + side}
+    above = {"seq": jnp.minimum(pair + 1, pairs - 1) * 2 + side}
 
     def mirror(level):
         apart = 1 << (level - local)
@@ -53,9 +46,15 @@
         return {"seq": (pair + apart - 2 * apart * bit) * 2 + side}
 
     barrier = pltpu.get_barrier_semaphore()
-    peers = [partner, below, above] + [mirror(l) for l in range(local, levels + 1)]
-    for peer in peers:
+
+    def greet(peer):
         pl.semaphore_signal(barrier, inc=1, device_id=peer, device_id_type=MESH)
+
+    greet(partner)
+    pl.when(jnp.logical_not(first))(lambda: greet(below))
+    pl.when(jnp.logical_not(last))(lambda: greet(above))
+    for level in range(local + 1, levels + 1):
+        greet(mirror(level))
 
     mine = pl.ds(pl.multiple_of(side * half, half), half)
     own_rows = pl.ds(pl.multiple_of(BLOCK + side * rows, BLOCK), rows)
@@ -67,7 +66,8 @@
     ]
     for load in loads:
         load.start()
-    pl.semaphore_wait(barrier, len(peers))
+    sides = jnp.where(first, 0, 1) + jnp.where(last, 0, 1)
+    pl.semaphore_wait(barrier, 1 + levels - local + sides)
 
     def lanes(h):
         return pl.ds(pl.multiple_of(h * HEAD_DIM, HEAD_DIM), HEAD_DIM)
@@ -128,10 +128,9 @@
         send_k(h).start()
         send_v(h).start()
 
-    each(start_kv)
-    each(lambda h: send_q(h).start())
-
-    first, last = pair == 0, pair == pairs - 1
+    ahead = min(2, heads)
+    for h in range(ahead):
+        start_kv(h)
 
     @pl.when(first)
     def _():
@@ -157,15 +156,15 @@
 
     rowid = lax.broadcasted_iota(jnp.int32, (BLOCK, 2 * BLOCK), 0)
     colid = lax.broadcasted_iota(jnp.int32, (BLOCK, 2 * BLOCK), 1)
-    averaging = jnp.where((colid >> 1) == rowid, 0.5, 0.0).astype(jnp.bfloat16)
-
-    def mean(x):
+    pairing = jnp.where((colid >> 1) == rowid, 1.0, 0.0).astype(jnp.bfloat16)
+
+    def pair_sum(x):
         count = x.shape[0]
         parts = []
         for at in range(0, count, 2 * BLOCK):
             size = min(2 * BLOCK, count - at)
             parts.append(
-                jnp.dot(averaging[: size // 2, :size], x[at : at + size],
+                jnp.dot(pairing[: size // 2, :size], x[at : at + size],
                         preferred_element_type=jnp.float32).astype(jnp.bfloat16)
             )
         return parts[0] if len(parts) == 1 else jnp.concatenate(parts, axis=0)
@@ -173,18 +172,28 @@
     def coarsen(h):
         send_k(h).wait_recv()
         send_v(h).wait_recv()
+
+        @pl.when(h + ahead < heads)
+        def _():
+            start_kv(h + ahead)
+
+        @pl.when(h + ahead >= heads)
+        def _():
+            for i in range(2):
+                send_q(2 * (h + ahead - heads) + i).start()
+
         halo(h, 1)
         both = jnp.concatenate(
             [kv[0, pl.ds(BLOCK, total), lanes(h)], kv[1, pl.ds(BLOCK, total), lanes(h)]],
             axis=1)
         offset = 0
         for level in range(1, local):
-            both = mean(both)
+            both = pair_sum(both)
             count = total >> level
             for t in range(2):
                 kv1[t, pl.ds(offset, count), lanes(h)] = both[:, t * HEAD_DIM : (t + 1) * HEAD_DIM]
             offset += count
-        both = mean(both)
+        both = pair_sum(both)
         for t in range(2):
             own[0, t, :, lanes(h)] = both[:, t * HEAD_DIM : (t + 1) * HEAD_DIM]
         send_level(local, h).start()
@@ -198,7 +207,7 @@
             send_level(level, h).wait_recv()
             for t in range(2):
                 joined = jnp.concatenate([own[at, t, :, lanes(h)], sib[at, t, :, lanes(h)]], axis=0)
-                own[at + 1, t, :, lanes(h)] = mean(joined)
+                own[at + 1, t, :, lanes(h)] = pair_sum(joined)
             send_level(level + 1, h).start()
 
         each(climb)
@@ -219,56 +228,55 @@
 
         queries = [qbuf[:, lanes(h)]]
         for level in range(1, levels + 1):
-            queries.append(mean(queries[-1]))
-
-        found = None
-        for level in range(levels, -1, -1):
-            count = total >> level
-            if level >= local:
-                at = level - local
-                tops, both = softmax_part(
-                    score(queries[level], sib[at, 0, :, lanes(h)]), sib[at, 1, :, lanes(h)])
-                pieces = [(0, count, tops, both)]
-            elif level >= 1:
-                offset = sum(total >> l for l in range(1, level))
-                pieces = []
-                for b in range(count // BLOCK):
-                    near = pl.ds(offset + (b ^ 1) * BLOCK, BLOCK)
-                    tops, both = softmax_part(
-                        score(queries[level][b * BLOCK : (b + 1) * BLOCK], kv1[0, near, lanes(h)]),
-                        kv1[1, near, lanes(h)])
-                    pieces.append((b * BLOCK, BLOCK, tops, both))
+            queries.append(pair_sum(queries[-1]))
+
+        def part(level, query, key, value, start, edge=None):
+            size = query.shape[0]
+            rate = RATE * 0.25**level
+            scores = score(query, key)
+            if edge is not None:
+                column, missing = edge
+                pieces = [scores[:, c : c + BLOCK] for c in range(0, scores.shape[1], BLOCK)]
+                pieces[column] = jnp.where(missing, -1e30, pieces[column])
+                scores = jnp.concatenate(pieces, axis=1)
+            top = jnp.max(scores, axis=1, keepdims=True) * rate
+            if level < levels:
+                span = pl.ds(start, size)
+                coarse_top = state[level, 0, span, :]
+                highest = jnp.maximum(jnp.broadcast_to(top, (size, HEAD_DIM)), coarse_top)
+                weight = jnp.exp2(coarse_top - highest)
             else:
-                pieces = []
-                for b in range(blocks):
-                    window = pl.ds(b * BLOCK, 3 * BLOCK)
-                    s = score(queries[0][b * BLOCK : (b + 1) * BLOCK], kv[0, window, lanes(h)])
-                    if b == 0:
-                        s = jnp.concatenate(
-                            [jnp.where(first, -1e30, s[:, :BLOCK]), s[:, BLOCK:]], axis=1)
-                    if b == blocks - 1:
-                        s = jnp.concatenate(
-                            [s[:, : 2 * BLOCK], jnp.where(last, -1e30, s[:, 2 * BLOCK :])], axis=1)
-                    tops, both = softmax_part(s, kv[1, window, lanes(h)])
-                    pieces.append((b * BLOCK, BLOCK, tops, both))
-            for start, size, tops, both in pieces:
-                num, den = both[:, :HEAD_DIM], both[:, HEAD_DIM:]
-                top = jnp.broadcast_to(tops, (size, HEAD_DIM))
-                if level < levels:
-                    span = pl.ds(start, size)
-                    coarse_top = state[level, 0, span, :]
-                    highest = jnp.maximum(top, coarse_top)
-                    fine_weight = jnp.exp2((top - highest) * RATE)
-                    coarse_weight = 2.0 * jnp.exp2((coarse_top - highest) * RATE)
-                    top = highest
-                    den = fine_weight * den + coarse_weight * state[level, 1, span, :]
-                    num = fine_weight * num + coarse_weight * state[level, 2, span, :]
-                if level == 0:
-                    obuf[pl.ds(start, size), lanes(h)] = (num / den).astype(obuf.dtype)
-                else:
-                    for at, x in enumerate((top, den, num)):
-                        for odd in range(2):
-                            state[level - 1, at, pl.ds(2 * start + odd, size, stride=2), :] = x
+                highest = jnp.broadcast_to(top, (size, HEAD_DIM))
+            wide = jnp.concatenate([highest] * (key.shape[0] // BLOCK), axis=1)
+            probs = jnp.exp2(scores * rate - wide).astype(jnp.bfloat16)
+            ones = jnp.full_like(value, 2.0**level)
+            both = jnp.dot(probs, jnp.concatenate([value, ones], axis=1),
+                           preferred_element_type=jnp.float32)
+            num, den = both[:, :HEAD_DIM], both[:, HEAD_DIM:]
+            if level < levels:
+                den = den + weight * state[level, 1, span, :]
+                num = num + weight * state[level, 2, span, :]
+            if level == 0:
+                obuf[pl.ds(start, size), lanes(h)] = (num / den).astype(obuf.dtype)
+            else:
+                for at, x in enumerate((highest, den, num)):
+                    for odd in range(2):
+                        state[level - 1, at, pl.ds(2 * start + odd, size, stride=2), :] = x
+
+        for level in range(levels, local - 1, -1):
+            at = level - local
+            part(level, queries[level], sib[at, 0, :, lanes(h)], sib[at, 1, :, lanes(h)], 0)
+        for level in range(local - 1, 0, -1):
+            offset = sum(total >> l for l in range(1, level))
+            for b in range((total >> level) // BLOCK):
+                near = pl.ds(offset + (b ^ 1) * BLOCK, BLOCK)
+                part(level, queries[level][b * BLOCK : (b + 1) * BLOCK],
+                     kv1[0, near, lanes(h)], kv1[1, near, lanes(h)], b * BLOCK)
+        for b in range(blocks):
+            window = pl.ds(b * BLOCK, 3 * BLOCK)
+            edge = (0, first) if b == 0 else (2, last) if b == blocks - 1 else None
+            part(0, queries[0][b * BLOCK : (b + 1) * BLOCK],
+                 kv[0, window, lanes(h)], kv[1, window, lanes(h)], b * BLOCK, edge)
         keep_out(h).start()
         send_out(h).start()
 
@@ -336,7 +344,7 @@
             dma((heads,)),
         ],
         compiler_params=pltpu.CompilerParams(
-            collective_id=0, has_side_effects=True, vmem_limit_bytes=40 * 2**20
+            collective_id=0, has_side_effects=True, vmem_limit_bytes=63 * 2**20
         ),
     )(queries, keys, values)
 

time: 45.5 us -> 42.3 us (0.930)
  local copies, waits for them, and re-layouts: 3.92 us -> 1.87 us
  Pallas kernels: 41.3 us -> 40.2 us
    unnamed x7 -> x1, local copies, waits for them, and re-layouts: 3.92 us -> 1.87 us
    pallas_call x1, Pallas kernels: 41.3 us -> 40.2 us  [on_device(): pl.pallas_call(functools.partial(kernel, pairs, levels, local), out_shape...]
where the time goes in v2:
time: 42.3 us; the launch traced here: 42.1 us
  Pallas kernels  40.2 us (95%)
  local copies, waits for them, and re-layouts  1.87 us (4%)
    pallas_call x1, Pallas kernels, on_device(): pl.pallas_call(functools.partial(kernel, pairs, levels, local), out_shape...  40.2 us
    unnamed x1, local copies, waits for them, and re-layouts  1.87 us

profile of v2, /device:TPU:0, one launch (start us, length us, event | category | flops | bytes accessed | tf_op | source)
XLA Modules:
  0.0 42.1 jit_solution(8629589168111693846)
XLA Ops:
  0.0 40.2 %shard_map.37 = bf16[256,1024]{1,0:T(8,128)(2,1)} custom-call(bf16[256,1024]{1,0:T(8,128)(2,1)} %q_in.1, bf16[256,1024]{1,0:T(8,128)(2,1)} %k_in.1, bf16[256,1024]{1,0:T(8,128)(2,1)} %v_in.1), custom_call_target="tpu_custom_call" | custom-call | tf_op jit(solution)/shard_map/pallas_call | solution.py:320
  40.2 1.9 %copy.5 = bf16[256,1024]{1,0:T(8,128)(2,1)} copy(bf16[256,1024]{1,0:T(8,128)(2,1)} %shard_map.37) | data formatting | bytes 1048576

commit v3 on v2

--- a/solution.py
+++ b/solution.py
@@ -198,19 +198,20 @@
             own[0, t, :, lanes(h)] = both[:, t * HEAD_DIM : (t + 1) * HEAD_DIM]
         send_level(local, h).start()
 
-    each(coarsen)
-
-    for level in range(local, levels):
+    def climb(level, h):
         at = level - local
-
-        def climb(h, level=level, at=at):
-            send_level(level, h).wait_recv()
-            for t in range(2):
-                joined = jnp.concatenate([own[at, t, :, lanes(h)], sib[at, t, :, lanes(h)]], axis=0)
-                own[at + 1, t, :, lanes(h)] = pair_sum(joined)
-            send_level(level + 1, h).start()
-
-        each(climb)
+        send_level(level, h).wait_recv()
+        for t in range(2):
+            joined = jnp.concatenate([own[at, t, :, lanes(h)], sib[at, t, :, lanes(h)]], axis=0)
+            own[at + 1, t, :, lanes(h)] = pair_sum(joined)
+        send_level(level + 1, h).start()
+
+    @pl.loop(0, heads + levels - local)
+    def _(step):
+        pl.when(step < heads)(lambda: coarsen(step))
+        for level in range(local, levels):
+            h = step - (level - local + 1)
+            pl.when((h >= 0) & (h < heads))(functools.partial(climb, level, h))
 
     loads[2].wait()
 

time: 42.3 us -> 40.7 us (0.962)
  Pallas kernels: 40.2 us -> 38.6 us
    pallas_call x1, Pallas kernels: 40.2 us -> 38.6 us  [on_device(): pl.pallas_call(functools.partial(kernel, pairs, levels, local), out_shape...]
where the time goes in v3:
time: 40.7 us; the launch traced here: 40.5 us
  Pallas kernels  38.6 us (95%)
  local copies, waits for them, and re-layouts  1.87 us (5%)
    pallas_call x1, Pallas kernels, on_device(): pl.pallas_call(functools.partial(kernel, pairs, levels, local), out_shape...  38.6 us
    unnamed x1, local copies, waits for them, and re-layouts  1.87 us

profile of v3, /device:TPU:0, one launch (start us, length us, event | category | flops | bytes accessed | tf_op | source)
XLA Modules:
  0.0 40.5 jit_solution(769678792372978779)
XLA Ops:
  0.0 38.6 %shard_map.37 = bf16[256,1024]{1,0:T(8,128)(2,1)} custom-call(bf16[256,1024]{1,0:T(8,128)(2,1)} %q_in.1, bf16[256,1024]{1,0:T(8,128)(2,1)} %k_in.1, bf16[256,1024]{1,0:T(8,128)(2,1)} %v_in.1), custom_call_target="tpu_custom_call" | custom-call | tf_op jit(solution)/shard_map/pallas_call | solution.py:321
  38.6 1.9 %copy.5 = bf16[256,1024]{1,0:T(8,128)(2,1)} copy(bf16[256,1024]{1,0:T(8,128)(2,1)} %shard_map.37) | data formatting | bytes 1048576
